TPU v7x, 32 devices: a whole 2x2x4 slice. The times are simulated.
32 devices in a mesh: row: 16 (over z, y, core), col: 2 (over x).
Axes of the slice: x: 2, y: 2, z: 4, core: 2. Of those that a mesh axis runs over, the one named last changes fastest.
Arguments:
- cells: bfloat16 [512, 1024, 128], P('row', 'col'), may hold values from -6 to 6
- upstream: bfloat16 [512, 1024, 128], P('row', 'col'), may hold values from -6 to 6
- counts: int32 [512], P('row'), may hold values from 1 to 1024, as said below
- key_weight: bfloat16 [128, 128], replicated, may hold values from -0.5 to 0.5
- value_weight: bfloat16 [128, 128], replicated, may hold values from -0.5 to 0.5
- out_weight: bfloat16 [128, 128], replicated, may hold values from -0.5 to 0.5
- row_query: float32 [128], replicated, may hold values from -60 to 60
- col_query: float32 [128], replicated, may hold values from -60 to 60
Outputs:
- cell_grad: bfloat16 [512, 1024, 128], P('row', 'col')
- key_weight_grad: float32 [128, 128], replicated
- value_weight_grad: float32 [128, 128], replicated
- out_weight_grad: float32 [128, 128], replicated
- row_query_grad: float32 [128], replicated
- col_query_grad: float32 [128], replicated
Inputs may be any that keep to these rules, and one draw needn't show every extreme that they name: `counts`: some row uses all 1024 columns and some row uses exactly one.
All inputs are finite; a program needn't handle non-finite values.
Results may differ from a plain program's by a relative error of at most 0.0047.
Values sent between devices are 32-bit elements; how exact they have to be, the bound alone decides.
A program may use at most 192 MiB of HBM per device.

v0:
```python
import functools
import math

import jax
import jax.numpy as jnp
from jax import lax
from jax.experimental import pallas as pl
from jax.experimental.pallas import tpu as pltpu
from jax.sharding import PartitionSpec as P

NEG_FILL = -1e30
HIGH = lax.Precision.HIGHEST
MESH = pl.DeviceIdType.MESH
F32 = jnp.float32
BF16 = jnp.bfloat16
VMEM_BYTES = 62 * 1024 * 1024


def dot_nt(a, b, precision=None):
    return lax.dot_general(
        a, b, (((1,), (1,)), ((), ())), precision=precision, preferred_element_type=F32
    )


def dot_tn(a, b, precision=None):
    return lax.dot_general(
        a, b, (((0,), (0,)), ((), ())), precision=precision, preferred_element_type=F32
    )


def dot_nn(a, b, precision=None):
    return jnp.dot(a, b, precision=precision, preferred_element_type=F32)


def split(x, parts):
    pieces = []
    for _ in range(parts):
        piece = x.astype(BF16).astype(F32)
        pieces.append(piece)
        x = x - piece
    return pieces


def stack_rows(rows, width):
    pad = jnp.zeros((16 - len(rows), width), F32)
    return jnp.concatenate(rows + [pad], 0).astype(BF16)


def flat_row(tile):
    return jnp.concatenate([tile[i : i + 1] for i in range(tile.shape[0])], 1)


def stats_kernel(
    n_row, n_col, chunk,
    cells_hbm, up_hbm, counts, wk_hbm, wv_hbm, wo_hbm, rq_hbm, cq_hbm,
    lhs_out, base_out, g_out, m_out, ab_out,
    cells, up, cot_loc, rs_buf, cot_full, row_cot, sr, sc, wr, wc, rdp, cdp,
    row_pool, row_grad, col_pool, row_buf, small, dots_buf, red_src, red_buf, part, m_full,
    ab_buf, ab_part, wk_ref, wv_ref, wo_ref, rq_ref, cq_ref,
    cell_sem, up_sem, in_sem, s_rs, r_rs, s_ag, r_ag, s_rx, r_rx, s_sm, r_sm, s_dt, r_dt,
    s_rd, r_rd, s_cx, r_cx, s_mg, r_mg, s_ab, r_ab, s_ac, r_ac,
):
    rows, cols, width = cells.shape
    scale = 1.0 / math.sqrt(width)
    me_r = lax.axis_index("row")
    me_c = lax.axis_index("col")
    n_chunk = rows // chunk
    per = cols // n_row
    m_per = width // n_row
    q_rows = cols // 128

    def local(hbm, vmem, sem, k):
        return pltpu.make_async_copy(
            hbm.at[pl.ds(k * chunk, chunk)], vmem.at[pl.ds(k * chunk, chunk)], sem.at[k]
        )

    for k in range(n_chunk):
        local(up_hbm, up, up_sem, k).start()
    small_in = [
        pltpu.make_async_copy(src, dst, in_sem.at[i])
        for i, (src, dst) in enumerate(
            ((wk_hbm, wk_ref), (wv_hbm, wv_ref), (wo_hbm, wo_ref), (rq_hbm, rq_ref), (cq_hbm, cq_ref))
        )
    ]
    for copy in small_in:
        copy.start()
    for k in range(n_chunk):
        local(cells_hbm, cells, cell_sem, k).start()
    sub16 = lax.broadcasted_iota(jnp.int32, (16, width), 0)

    barrier = pltpu.get_barrier_semaphore()

    @pl.loop(1, n_row)
    def _(d):
        pl.semaphore_signal(
            barrier, inc=1, device_id=(lax.rem(me_r + d, n_row), me_c), device_id_type=MESH
        )

    @pl.loop(1, n_col)
    def _(d):
        pl.semaphore_signal(
            barrier, inc=1, device_id=(me_r, lax.rem(me_c + d, n_col)), device_id_type=MESH
        )

    def to_rows(src_of, dst, s_sem, r_sem, d):
        peer = lax.rem(me_r + d, n_row)
        return pltpu.make_async_remote_copy(
            src_ref=src_of(peer), dst_ref=dst.at[me_r], send_sem=s_sem.at[d],
            recv_sem=r_sem.at[d], device_id=(peer, me_c), device_id_type=MESH,
        )

    def from_rows(src_of, dst, s_sem, r_sem, d):
        peer = lax.rem(me_r + n_row - d, n_row)
        return pltpu.make_async_remote_copy(
            src_ref=src_of(peer), dst_ref=dst.at[peer], send_sem=s_sem.at[d],
            recv_sem=r_sem.at[d], device_id=(peer, me_c), device_id_type=MESH,
        )

    def to_cols(src, dst, s_sem, r_sem, d):
        peer = lax.rem(me_c + d, n_col)
        return pltpu.make_async_remote_copy(
            src_ref=src, dst_ref=dst.at[me_c], send_sem=s_sem.at[d],
            recv_sem=r_sem.at[d], device_id=(me_r, peer), device_id_type=MESH,
        )

    def from_cols(src, dst, s_sem, r_sem, d):
        peer = lax.rem(me_c + n_col - d, n_col)
        return pltpu.make_async_remote_copy(
            src_ref=src, dst_ref=dst.at[peer], send_sem=s_sem.at[d],
            recv_sem=r_sem.at[d], device_id=(me_r, peer), device_id_type=MESH,
        )

    def start_rows(*args):
        @pl.loop(1, n_row)
        def _(d):
            to_rows(*args, d).start()

    def wait_rows(*args):
        @pl.loop(1, n_row)
        def _(d):
            to_rows(*args, d).wait_send()
            from_rows(*args, d).wait_recv()

    def start_cols(*args):
        @pl.loop(1, n_col)
        def _(d):
            to_cols(*args, d).start()

    def wait_cols(*args):
        @pl.loop(1, n_col)
        def _(d):
            to_cols(*args, d).wait_send()
            from_cols(*args, d).wait_recv()

    span = 64
    groups = span // per
    for k in range(n_chunk):
        local(up_hbm, up, up_sem, k).wait()

        def add_block(cb, total, k=k):
            x = up[pl.ds(k * chunk, chunk), pl.ds(pl.multiple_of(cb * span, span), span), :]
            x = x.astype(F32)
            by_col = jnp.sum(x, 0).reshape(groups, per, width)
            at = pl.ds(cb * groups, groups)
            cot_loc[at] = by_col if k == 0 else cot_loc[at] + by_col
            return total + jnp.sum(x, 1)

        row_cot[pl.ds(k * chunk, chunk), :] = lax.fori_loop(
            0, cols // span, add_block, jnp.zeros((chunk, width), F32)
        )

    pl.semaphore_wait(barrier, n_row + n_col - 2)
    scatter = (lambda peer: cot_loc.at[peer], rs_buf, s_rs, r_rs)
    start_rows(*scatter)
    rs_buf[me_r] = cot_loc[me_r]

    for copy in small_in:
        copy.wait()
    wk = wk_ref[...].astype(F32)
    queries = jnp.concatenate([rq_ref[...], cq_ref[...], jnp.zeros((6, width), F32)], 0)
    kvec = dot_nt(queries, wk, HIGH) * scale
    kr, kc = kvec[0:1], kvec[1:2]
    k_pieces = stack_rows(split(kr, 3) + split(kc, 3), width)
    ids = me_c * cols + lax.broadcasted_iota(jnp.int32, (1, cols), 1)

    @pl.loop(0, n_chunk)
    def _(k):
        local(cells_hbm, cells, cell_sem, k).wait()
        at = pl.ds(pl.multiple_of(k * chunk, chunk), chunk)
        s = dot_nt(k_pieces, cells[at].reshape(chunk * cols, width))
        one, two = [], []
        for i in range(chunk):
            x = s[:, i * cols : (i + 1) * cols]
            live = ids < counts[k * chunk + i]
            one.append(jnp.where(live, x[0:1] + x[1:2] + x[2:3], NEG_FILL))
            two.append(jnp.where(live, x[3:4] + x[4:5] + x[5:6], NEG_FILL))
        sr[at, :] = jnp.concatenate(one, 0)
        sc[at, :] = jnp.concatenate(two, 0)

    wait_rows(*scatter)
    own = rs_buf[0]
    for i in range(1, n_row):
        own = own + rs_buf[i]
    cot_full[me_r] = own
    gather = (lambda peer: cot_full.at[me_r], cot_full, s_ag, r_ag)
    start_rows(*gather)

    score = sc[...]
    col_m = jnp.max(score, 0, keepdims=True)
    weight = jnp.where(score > 0.5 * NEG_FILL, jnp.exp(score - col_m), 0.0)
    wc[...] = weight
    col_t = jnp.sum(weight, 0, keepdims=True)
    for j, value in enumerate((col_m, col_t)):
        for i in range(q_rows):
            small[me_r, pl.ds(j * q_rows + i, 1), :] = value[:, i * 128 : (i + 1) * 128]
    small_x = (lambda peer: small.at[me_r], small, s_sm, r_sm)
    start_rows(*small_x)

    score = sr[...]
    row_m = jnp.max(score, 1, keepdims=True)
    row_weight = jnp.where(score > 0.5 * NEG_FILL, jnp.exp(score - row_m), 0.0)
    wr[...] = row_weight
    row_t = jnp.sum(row_weight, 1, keepdims=True)
    sub = lax.broadcasted_iota(jnp.int32, (chunk, 1), 0)

    @pl.loop(0, n_chunk)
    def _(k):
        at = pl.ds(pl.multiple_of(k * chunk, chunk), chunk)
        pieces = jnp.concatenate(split(wr[at, :], 2), 0).astype(BF16)
        acc = jnp.zeros((chunk, width), F32)
        for i in range(chunk):
            s = jnp.dot(pieces, cells[k * chunk + i], preferred_element_type=F32)
            acc = jnp.where(sub == i, s[0:chunk] + s[chunk : 2 * chunk], acc)
        row_pool[at, :] = acc

    row_buf[me_c, 0] = row_pool[...]
    row_buf[me_c, 1] = row_cot[...]
    row_buf[me_c, 2] = jnp.broadcast_to(row_m, (rows, width))
    row_buf[me_c, 3] = jnp.broadcast_to(row_t, (rows, width))
    row_x = (row_buf.at[me_c], row_buf, s_rx, r_rx)
    start_cols(*row_x)

    w_t = jnp.concatenate([p.T for p in split(weight, 2)], 1).astype(BF16)
    pick = lax.rem(lax.broadcasted_iota(jnp.int32, (2 * rows, 2 * width), 0), rows)
    lane = lax.broadcasted_iota(jnp.int32, (2 * rows, 2 * width), 1)
    pick = pick - jnp.where(lane < width, 0, 1)
    col_pool[...] = jnp.zeros_like(col_pool)

    @pl.loop(0, rows // 4)
    def _(k):
        acc = col_pool[...]
        for i in (0, 2):
            r = k * 4 + i
            one = jnp.where(pick == r, 1.0, 0.0).astype(BF16)
            spread = jnp.dot(w_t, one, preferred_element_type=F32)
            acc = acc + spread[:, :width] * cells[r].astype(F32)
            acc = acc + spread[:, width:] * cells[r + 1].astype(F32)
        col_pool[...] = acc

    wait_cols(*row_x)
    top = row_buf[0, 2]
    for i in range(1, n_col):
        top = jnp.maximum(top, row_buf[i, 2])
    pool = jnp.zeros((rows, width), F32)
    total = jnp.zeros((rows, width), F32)
    cot = jnp.zeros((rows, width), F32)
    for i in range(n_col):
        decay = jnp.exp(row_buf[i, 2] - top)
        pool = pool + row_buf[i, 0] * decay
        total = total + row_buf[i, 3] * decay
        cot = cot + row_buf[i, 1]
    factor = jnp.exp(row_buf[me_c, 2] - top) / total
    both = jnp.dot(wv_ref[...], wo_ref[...], preferred_element_type=F32)
    g_row = dot_nt(cot, both, HIGH)
    row_grad[...] = g_row
    row_dot = jnp.sum(pool * g_row, 1, keepdims=True) / total[:, 0:1]
    row_prob = wr[...] * factor[:, 0:1]

    @pl.loop(0, n_chunk)
    def _(k):
        at = pl.ds(pl.multiple_of(k * chunk, chunk), chunk)
        pieces = jnp.concatenate(split(row_grad[at, :], 2), 0).astype(BF16)
        acc = jnp.zeros((chunk, cols), F32)
        for i in range(chunk):
            s = dot_nt(pieces, cells[k * chunk + i])
            acc = jnp.where(sub == i, s[0:chunk] + s[chunk : 2 * chunk], acc)
        rdp[at, :] = acc

    row_ds = row_prob * (rdp[...] - row_dot)
    sr[...] = row_ds

    wait_rows(*small_x)
    top = small[0, 0:q_rows]
    for i in range(1, n_row):
        top = jnp.maximum(top, small[i, 0:q_rows])
    total = jnp.zeros((q_rows, 128), F32)
    for i in range(n_row):
        total = total + small[i, q_rows : 2 * q_rows] * jnp.exp(small[i, 0:q_rows] - top)
    f_col = jnp.exp(col_m - flat_row(top)) / flat_row(total)
    col_prob = wc[...] * f_col
    wc[...] = col_prob
    f_t = jnp.broadcast_to(f_col, (8, cols)).T[:, 0:1]

    wait_rows(*gather)
    cot_all = cot_full[...].reshape(cols, width)
    m_loc = dot_tn(col_pool[...] * f_t, cot_all, HIGH)
    m_loc = m_loc + dot_tn(row_pool[...] * factor, cot, HIGH)
    for i in range(n_row):
        red_src[i, 0:m_per] = m_loc[i * m_per : (i + 1) * m_per]
        if m_per < 8:
            red_src[i, m_per:8] = jnp.zeros((8 - m_per, width), F32)
    reduce = (lambda peer: red_src.at[peer], red_buf, s_rd, r_rd)
    start_rows(*reduce)
    red_buf[me_r] = red_src[me_r]

    g_col = dot_nt(cot_all, both, HIGH)
    g_out[...] = g_col

    @pl.loop(0, n_chunk)
    def _(k):
        at = pl.ds(pl.multiple_of(k * chunk, chunk), chunk)
        acc = jnp.zeros((16, cols), F32)
        for i in range(chunk):
            prod = cells[k * chunk + i].astype(F32) * g_out[...]
            hi = prod.astype(BF16)
            lo = (prod - hi.astype(F32)).astype(BF16)
            ones = jnp.where(sub16 == i, 1.0, 0.0).astype(BF16)
            acc = acc + dot_nt(ones, hi) + dot_nt(ones, lo)
        cdp[at, :] = acc[0:chunk]

    part_dot = jnp.sum(wc[...] * cdp[...], 0, keepdims=True)
    for i in range(q_rows):
        dots_buf[me_r, pl.ds(i, 1), :] = part_dot[:, i * 128 : (i + 1) * 128]
    dots_x = (lambda peer: dots_buf.at[me_r], dots_buf, s_dt, r_dt)
    start_rows(*dots_x)

    wait_rows(*reduce)
    acc = red_buf[0]
    for i in range(1, n_row):
        acc = acc + red_buf[i]
    part[me_c] = acc
    col_x = (part.at[me_c], part, s_cx, r_cx)
    start_cols(*col_x)

    wait_rows(*dots_x)
    dots = dots_buf[0, 0:q_rows]
    for i in range(1, n_row):
        dots = dots + dots_buf[i, 0:q_rows]
    col_ds = wc[...] * (cdp[...] - flat_row(dots))
    sc[...] = col_ds

    turn = lax.rem(lax.broadcasted_iota(jnp.int32, (4 * chunk, 1), 0), chunk)

    def moments(k, acc):
        at = pl.ds(pl.multiple_of(k * chunk, chunk), chunk)
        pieces = split(sr[at, :], 2) + split(sc[at, :], 2)
        pieces = jnp.concatenate(pieces, 0).astype(BF16)
        for i in range(chunk):
            s = jnp.dot(pieces, cells[k * chunk + i], preferred_element_type=F32)
            acc = acc + jnp.where(turn == i, s, 0.0)
        return acc

    acc = lax.fori_loop(0, n_chunk, moments, jnp.zeros((4 * chunk, width), F32))
    ab_buf[me_r] = jnp.concatenate(
        [
            jnp.sum(acc[0 : 2 * chunk], 0, keepdims=True),
            jnp.sum(acc[2 * chunk : 4 * chunk], 0, keepdims=True),
            jnp.zeros((6, width), F32),
        ],
        0,
    )
    ab_x = (lambda peer: ab_buf.at[me_r], ab_buf, s_ab, r_ab)
    start_rows(*ab_x)

    wait_cols(*col_x)
    acc = part[0]
    for i in range(1, n_col):
        acc = acc + part[i]
    m_full[me_r] = acc
    collect = (lambda peer: m_full.at[me_r], m_full, s_mg, r_mg)
    start_rows(*collect)

    pieces = [split(x, 2) for x in (row_prob, row_ds, col_ds, wc[...])]
    for half in range(2):
        block = jnp.concatenate([p[half] for p in pieces], 0)
        lhs_out[:, half * 4 * rows : (half + 1) * 4 * rows] = block.T.astype(BF16)
    zero = jnp.zeros((rows, width), F32)
    one = jnp.ones((rows, width), F32)
    left = jnp.concatenate(
        [g_row, jnp.broadcast_to(kr, (rows, width)), jnp.broadcast_to(kc, (rows, width)), zero], 0
    )
    right = jnp.concatenate([zero, zero, zero, one], 0)
    half = jnp.concatenate([left, right], 1)
    base_out[...] = jnp.concatenate([half, half], 0)

    wait_rows(*ab_x)
    acc = ab_buf[0]
    for i in range(1, n_row):
        acc = acc + ab_buf[i]
    ab_part[me_c] = acc
    ab_cx = (ab_part.at[me_c], ab_part, s_ac, r_ac)
    start_cols(*ab_cx)
    wait_rows(*collect)
    m_out[...] = jnp.concatenate([m_full[i, 0:m_per] for i in range(n_row)], 0)
    wait_cols(*ab_cx)
    acc = ab_part[0]
    for i in range(1, n_col):
        acc = acc + ab_part[i]
    ab_out[...] = acc


def cell_kernel(
    rows, lhs_ref, base_ref, g_ref, m_ref, ab_ref, wk_ref, wv_ref, wo_ref, rq_ref, cq_ref, up_ref,
    out_ref, kwg_ref, vwg_ref, owg_ref, rqg_ref, cqg_ref,
):
    block = up_ref.shape[0]
    width = up_ref.shape[2]
    step = pl.program_id(0)
    scale = 1.0 / math.sqrt(width)
    owner = lax.rem(lax.broadcasted_iota(jnp.int32, base_ref.shape, 0), rows)

    @pl.when(step == 0)
    def _():
        ab, m = ab_ref[...], m_ref[...]
        queries = jnp.concatenate([rq_ref[...], cq_ref[...], jnp.zeros((6, width), F32)], 0)
        kwg_ref[...] = dot_tn(ab, queries * scale, HIGH)
        q_grad = dot_nn(ab, wk_ref[...].astype(F32), HIGH) * scale
        rqg_ref[...] = q_grad[0:1]
        cqg_ref[...] = q_grad[1:2]
        vwg_ref[...] = dot_nt(m, wo_ref[...].astype(F32), HIGH)
        owg_ref[...] = dot_tn(wv_ref[...].astype(F32), m, HIGH)

    @pl.loop(0, block, unroll=4)
    def _(i):
        rhs = jnp.where(owner == step * block + i, base_ref[...], 0.0).astype(BF16)
        res = jnp.dot(lhs_ref[...], rhs, preferred_element_type=F32)
        delta = res[:, :width] + res[:, width:] * g_ref[...]
        out_ref[i] = (up_ref[i].astype(F32) + delta).astype(out_ref.dtype)


def on_device(n_row, n_col, cells, upstream, counts, wk, wv, wo, rq, cq):
    rows, cols, width = cells.shape
    chunk = 8
    per = cols // n_row
    rq, cq = rq.reshape(1, width), cq.reshape(1, width)
    vmem = pl.BlockSpec(memory_space=pltpu.VMEM)
    hbm = pl.BlockSpec(memory_space=pl.ANY)
    n_chunk = rows // chunk
    dma = pltpu.SemaphoreType.DMA
    f32 = lambda *shape: pltpu.VMEM(shape, F32)
    small_rows = -(-2 * (cols // 128) // 8) * 8
    dots_rows = -(-(cols // 128) // 8) * 8
    square = jax.ShapeDtypeStruct((width, width), F32)
    vector = jax.ShapeDtypeStruct((1, width), F32)
    over_row, over_col = dma((n_row,)), dma((n_col,))
    lhs, base, g_col, m, ab = pl.pallas_call(
        functools.partial(stats_kernel, n_row, n_col, chunk),
        out_shape=(
            jax.ShapeDtypeStruct((cols, 8 * rows), BF16),
            jax.ShapeDtypeStruct((8 * rows, 2 * width), F32),
            jax.ShapeDtypeStruct((cols, width), F32),
            square,
            jax.ShapeDtypeStruct((8, width), F32),
        ),
        in_specs=[hbm, hbm, pl.BlockSpec(memory_space=pltpu.SMEM)] + [hbm] * 5,
        out_specs=(vmem,) * 5,
        scratch_shapes=[
            pltpu.VMEM(cells.shape, BF16), pltpu.VMEM(cells.shape, BF16),
            f32(n_row, per, width), f32(n_row, per, width), f32(n_row, per, width),
            f32(rows, width),
            f32(rows, cols), f32(rows, cols), f32(rows, cols), f32(rows, cols),
            f32(rows, cols), f32(rows, cols),
            f32(rows, width), f32(rows, width), f32(cols, width),
            f32(n_col, 4, rows, width),
            f32(n_row, small_rows, 128), f32(n_row, dots_rows, 128),
            f32(n_row, 8, width), f32(n_row, 8, width), f32(n_col, 8, width),
            f32(n_row, 8, width),
            f32(n_row, 8, width), f32(n_col, 8, width),
            pltpu.VMEM(wk.shape, BF16), pltpu.VMEM(wv.shape, BF16), pltpu.VMEM(wo.shape, BF16),
            f32(1, width), f32(1, width),
            dma((n_chunk,)), dma((n_chunk,)), dma((5,)),
            over_row, over_row, over_row, over_row,
            over_col, over_col, over_row, over_row, over_row, over_row,
            over_row, over_row, over_col, over_col, over_row, over_row,
            over_row, over_row, over_col, over_col,
        ],
        compiler_params=pltpu.CompilerParams(
            collective_id=0, has_side_effects=True, vmem_limit_bytes=VMEM_BYTES
        ),
        name="hub_stats",
    )(cells, upstream, counts, wk, wv, wo, rq, cq)
    block = 8
    whole = lambda shape: pl.BlockSpec(shape, lambda i: (0,) * len(shape))
    cell_spec = pl.BlockSpec((block, cols, width), lambda i: (i, 0, 0))
    fixed = (lhs, base, g_col, m, ab, wk, wv, wo, rq, cq)
    cell_grad, kwg, vwg, owg, rqg, cqg = pl.pallas_call(
        functools.partial(cell_kernel, rows),
        grid=(rows // block,),
        out_shape=(
            jax.ShapeDtypeStruct(cells.shape, cells.dtype),
            square, square, square, vector, vector,
        ),
        in_specs=[whole(x.shape) for x in fixed] + [cell_spec],
        out_specs=(cell_spec,) + (whole((width, width)),) * 3 + (whole((1, width)),) * 2,
        compiler_params=pltpu.CompilerParams(vmem_limit_bytes=VMEM_BYTES),
        name="cell_grad",
    )(*fixed, upstream)
    return cell_grad, kwg, vwg, owg, rqg.reshape(width), cqg.reshape(width)


def solution(mesh):
    placed = (P("row", "col", None), P("row", "col", None), P("row"), P(), P(), P(), P(), P())
    return jax.shard_map(
        functools.partial(on_device, mesh.shape["row"], mesh.shape["col"]),
        mesh=mesh,
        in_specs=placed,
        out_specs=(P("row", "col", None), P(), P(), P(), P(), P()),
        check_vma=False,
    )
```

profile of v0, /device:TPU:0, one launch (start us, length us, event | category | flops | bytes accessed | tf_op | source)
XLA Modules:
  0.0 51.5 jit_solution(14217915552866086975)
XLA Ops:
  0.6 43.3 %hub_stats.1 = (bf16[512,256]{1,0:T(8,128)(2,1)}, f32[256,256]{1,0:T(8,128)}, f32[512,128]{1,0:T(8,128)}, f32[128,128]{1,0:T(8,128)}, f32[8,128]{1,0:T(8,128)}) custom-call(bf16[32,512,128]{2,1,0:T(8,128)(2,1)} %cells_hbm.1, bf16[32,512,128]{2,1,0:T(8,128)(2,1)} %up_ref.1, s32[32]{0:T(128)} %counts.1, bf16[128,128]{1,0:T(8,128)(2,1)} %wk_ref.1, ...), custom_call_target="tpu_custom_call" | custom-call | tf_op jit(solution)/shard_map/hub_stats/pallas_call | solution.py:456
  44.0 7.5 %cell_grad.1 = (bf16[32,512,128]{2,1,0:T(8,128)(2,1)}, f32[128,128]{1,0:T(8,128)}, f32[128,128]{1,0:T(8,128)}, f32[128,128]{1,0:T(8,128)}, f32[1,128]{1,0:T(1,128)}, /*index=5*/f32[1,128]{1,0:T(1,128)}) custom-call(bf16[512,256]{1,0:T(8,128)(2,1)} %get-tuple-element.17.lhs_ref, f32[256,256]{1,0:T(8,128)} %get-tuple-element.18.base_ref, ...), custom_call_target="tpu_custom_call" | custom-call | tf_op jit(solution)/shard_map/cell_grad/pallas_call | solution.py:496
where the time goes:
time: 51.7 us; the launch traced here: 51.5 us
  Pallas kernels  50.8 us (98%)
  between operations  0.64 us (1%)
    pallas_call x1, Pallas kernels, on_device(): pl.pallas_call(functools.partial(stats_kernel, n_row, n_col, chunk), out_...  43.3 us
    pallas_call x1, Pallas kernels, on_device(): pl.pallas_call(functools.partial(cell_kernel, rows), grid=(rows // block,...  7.5 us

commit v1 on v0

--- a/solution.py
+++ b/solution.py
@@ -54,10 +54,10 @@
     n_row, n_col, chunk,
     cells_hbm, up_hbm, counts, wk_hbm, wv_hbm, wo_hbm, rq_hbm, cq_hbm,
     lhs_out, base_out, g_out, m_out, ab_out,
-    cells, up, cot_loc, rs_buf, cot_full, row_cot, sr, sc, wr, wc, rdp, cdp,
+    cells, up, cot_loc, pair_buf, chip_sum, rs_buf, cot_full, row_cot, sr, sc, wr, wc, rdp, cdp,
     row_pool, row_grad, col_pool, row_buf, small, dots_buf, red_src, red_buf, part, m_full,
     ab_buf, ab_part, wk_ref, wv_ref, wo_ref, rq_ref, cq_ref,
-    cell_sem, up_sem, in_sem, s_rs, r_rs, s_ag, r_ag, s_rx, r_rx, s_sm, r_sm, s_dt, r_dt,
+    cell_sem, up_sem, in_sem, s_pr, r_pr, s_rs, r_rs, s_ag, r_ag, s_rx, r_rx, s_sm, r_sm, s_dt, r_dt,
     s_rd, r_rd, s_cx, r_cx, s_mg, r_mg, s_ab, r_ab, s_ac, r_ac,
 ):
     rows, cols, width = cells.shape
@@ -130,6 +130,30 @@
             recv_sem=r_sem.at[d], device_id=(me_r, peer), device_id_type=MESH,
         )
 
+    half_n = n_row // 2
+    me_core, me_chip = lax.rem(me_r, 2), lax.div(me_r, 2)
+    mine, other = me_core * half_n, (1 - me_core) * half_n
+
+    def to_sibling(src, dst, s_sem, r_sem):
+        return pltpu.make_async_remote_copy(
+            src_ref=src, dst_ref=dst, send_sem=s_sem, recv_sem=r_sem,
+            device_id=(me_r + 1 - 2 * me_core, me_c), device_id_type=MESH,
+        )
+
+    def to_chips(src_of, dst, s_sem, r_sem, d):
+        chip = lax.rem(me_chip + d, half_n)
+        return pltpu.make_async_remote_copy(
+            src_ref=src_of(chip), dst_ref=dst, send_sem=s_sem.at[d], recv_sem=r_sem.at[d],
+            device_id=(chip * 2 + me_core, me_c), device_id_type=MESH,
+        )
+
+    def from_chips(dst_of, s_sem, r_sem, d):
+        chip = lax.rem(me_chip + half_n - d, half_n)
+        return pltpu.make_async_remote_copy(
+            src_ref=dst_of(chip), dst_ref=dst_of(chip), send_sem=s_sem.at[d],
+            recv_sem=r_sem.at[d], device_id=(chip * 2 + me_core, me_c), device_id_type=MESH,
+        )
+
     def start_rows(*args):
         @pl.loop(1, n_row)
         def _(d):
@@ -170,9 +194,8 @@
         )
 
     pl.semaphore_wait(barrier, n_row + n_col - 2)
-    scatter = (lambda peer: cot_loc.at[peer], rs_buf, s_rs, r_rs)
-    start_rows(*scatter)
-    rs_buf[me_r] = cot_loc[me_r]
+    swap = to_sibling(cot_loc.at[pl.ds(other, half_n)], pair_buf, s_pr.at[0], r_pr.at[0])
+    swap.start()
 
     for copy in small_in:
         copy.wait()
@@ -182,6 +205,14 @@
     kr, kc = kvec[0:1], kvec[1:2]
     k_pieces = stack_rows(split(kr, 3) + split(kc, 3), width)
     ids = me_c * cols + lax.broadcasted_iota(jnp.int32, (1, cols), 1)
+
+    swap.wait()
+    chip_sum[...] = cot_loc[pl.ds(mine, half_n)] + pair_buf[...]
+    rs_buf[me_chip] = chip_sum[me_chip]
+
+    @pl.loop(1, half_n)
+    def _(d):
+        to_chips(lambda chip: chip_sum.at[chip], rs_buf.at[me_chip], s_rs, r_rs, d).start()
 
     @pl.loop(0, n_chunk)
     def _(k):
@@ -197,13 +228,21 @@
         sr[at, :] = jnp.concatenate(one, 0)
         sc[at, :] = jnp.concatenate(two, 0)
 
-    wait_rows(*scatter)
+    @pl.loop(1, half_n)
+    def _(d):
+        to_chips(lambda chip: chip_sum.at[chip], rs_buf.at[me_chip], s_rs, r_rs, d).wait_send()
+        from_chips(lambda chip: rs_buf.at[chip], s_rs, r_rs, d).wait_recv()
+
     own = rs_buf[0]
-    for i in range(1, n_row):
+    for i in range(1, half_n):
         own = own + rs_buf[i]
-    cot_full[me_r] = own
-    gather = (lambda peer: cot_full.at[me_r], cot_full, s_ag, r_ag)
-    start_rows(*gather)
+    cot_full[mine + me_chip] = own
+    own_slot = cot_full.at[mine + me_chip]
+
+    @pl.loop(1, half_n)
+    def _(d):
+        to_chips(lambda chip: own_slot, own_slot, s_ag, r_ag, d).start()
+
 
     score = sc[...]
     col_m = jnp.max(score, 0, keepdims=True)
@@ -276,6 +315,15 @@
     row_dot = jnp.sum(pool * g_row, 1, keepdims=True) / total[:, 0:1]
     row_prob = wr[...] * factor[:, 0:1]
 
+    @pl.loop(1, half_n)
+    def _(d):
+        to_chips(lambda chip: own_slot, own_slot, s_ag, r_ag, d).wait_send()
+        from_chips(lambda chip: cot_full.at[mine + chip], s_ag, r_ag, d).wait_recv()
+
+    half_at = cot_full.at[pl.ds(mine, half_n)]
+    fill = to_sibling(half_at, half_at, s_pr.at[1], r_pr.at[1])
+    fill.start()
+
     @pl.loop(0, n_chunk)
     def _(k):
         at = pl.ds(pl.multiple_of(k * chunk, chunk), chunk)
@@ -301,7 +349,9 @@
     wc[...] = col_prob
     f_t = jnp.broadcast_to(f_col, (8, cols)).T[:, 0:1]
 
-    wait_rows(*gather)
+    fill.wait_send()
+    other_at = cot_full.at[pl.ds(other, half_n)]
+    to_sibling(other_at, other_at, s_pr.at[1], r_pr.at[1]).wait_recv()
     cot_all = cot_full[...].reshape(cols, width)
     m_loc = dot_tn(col_pool[...] * f_t, cot_all, HIGH)
     m_loc = m_loc + dot_tn(row_pool[...] * factor, cot, HIGH)
@@ -452,7 +502,8 @@
     dots_rows = -(-(cols // 128) // 8) * 8
     square = jax.ShapeDtypeStruct((width, width), F32)
     vector = jax.ShapeDtypeStruct((1, width), F32)
-    over_row, over_col = dma((n_row,)), dma((n_col,))
+    half_n = n_row // 2
+    over_row, over_col, over_chip = dma((n_row,)), dma((n_col,)), dma((half_n,))
     lhs, base, g_col, m, ab = pl.pallas_call(
         functools.partial(stats_kernel, n_row, n_col, chunk),
         out_shape=(
@@ -466,7 +517,8 @@
         out_specs=(vmem,) * 5,
         scratch_shapes=[
             pltpu.VMEM(cells.shape, BF16), pltpu.VMEM(cells.shape, BF16),
-            f32(n_row, per, width), f32(n_row, per, width), f32(n_row, per, width),
+            f32(n_row, per, width), f32(half_n, per, width), f32(half_n, per, width),
+            f32(half_n, per, width), f32(n_row, per, width),
             f32(rows, width),
             f32(rows, cols), f32(rows, cols), f32(rows, cols), f32(rows, cols),
             f32(rows, cols), f32(rows, cols),
@@ -478,8 +530,8 @@
             f32(n_row, 8, width), f32(n_col, 8, width),
             pltpu.VMEM(wk.shape, BF16), pltpu.VMEM(wv.shape, BF16), pltpu.VMEM(wo.shape, BF16),
             f32(1, width), f32(1, width),
-            dma((n_chunk,)), dma((n_chunk,)), dma((5,)),
-            over_row, over_row, over_row, over_row,
+            dma((n_chunk,)), dma((n_chunk,)), dma((5,)), dma((2,)), dma((2,)),
+            over_chip, over_chip, over_chip, over_chip,
             over_col, over_col, over_row, over_row, over_row, over_row,
             over_row, over_row, over_col, over_col, over_row, over_row,
             over_row, over_row, over_col, over_col,

time: 51.7 us -> 48.2 us (0.932)
  Pallas kernels: 50.8 us -> 47.4 us
    pallas_call x1, Pallas kernels: 43.3 us -> 39.9 us  [on_device(): pl.pallas_call(functools.partial(stats_kernel, n_row, n_col, chunk), out_...]
where the time goes in v1:
time: 48.2 us; the launch traced here: 48 us
  Pallas kernels  47.4 us (98%)
  between operations  0.64 us (1%)
    pallas_call x1, Pallas kernels, on_device(): pl.pallas_call(functools.partial(stats_kernel, n_row, n_col, chunk), out_...  39.9 us
    pallas_call x1, Pallas kernels, on_device(): pl.pallas_call(functools.partial(cell_kernel, rows), grid=(rows // block,...  7.5 us

profile of v1, /device:TPU:0, one launch (start us, length us, event | category | flops | bytes accessed | tf_op | source)
XLA Modules:
  0.0 48.0 jit_solution(332210733285235823)
XLA Ops:
  0.6 39.9 %hub_stats.1 = (bf16[512,256]{1,0:T(8,128)(2,1)}, f32[256,256]{1,0:T(8,128)}, f32[512,128]{1,0:T(8,128)}, f32[128,128]{1,0:T(8,128)}, f32[8,128]{1,0:T(8,128)}) custom-call(bf16[32,512,128]{2,1,0:T(8,128)(2,1)} %cells_hbm.1, bf16[32,512,128]{2,1,0:T(8,128)(2,1)} %up_ref.1, s32[32]{0:T(128)} %counts.1, bf16[128,128]{1,0:T(8,128)(2,1)} %wk_ref.1, ...), custom_call_target="tpu_custom_call" | custom-call | tf_op jit(solution)/shard_map/hub_stats/pallas_call | solution.py:507
  40.5 7.5 %cell_grad.1 = (bf16[32,512,128]{2,1,0:T(8,128)(2,1)}, f32[128,128]{1,0:T(8,128)}, f32[128,128]{1,0:T(8,128)}, f32[128,128]{1,0:T(8,128)}, f32[1,128]{1,0:T(1,128)}, /*index=5*/f32[1,128]{1,0:T(1,128)}) custom-call(bf16[512,256]{1,0:T(8,128)(2,1)} %get-tuple-element.17.lhs_ref, f32[256,256]{1,0:T(8,128)} %get-tuple-element.18.base_ref, ...), custom_call_target="tpu_custom_call" | custom-call | tf_op jit(solution)/shard_map/cell_grad/pallas_call | solution.py:548

commit v2 on v1

--- a/solution.py
+++ b/solution.py
@@ -53,11 +53,12 @@
 def stats_kernel(
     n_row, n_col, chunk,
     cells_hbm, up_hbm, counts, wk_hbm, wv_hbm, wo_hbm, rq_hbm, cq_hbm,
-    lhs_out, base_out, g_out, m_out, ab_out,
+    raw_hbm, m_out, ab_out,
+    lhs_out, base_out, g_out,
     cells, up, cot_loc, pair_buf, chip_sum, rs_buf, cot_full, row_cot, sr, sc, wr, wc, rdp, cdp,
     row_pool, row_grad, col_pool, row_buf, small, dots_buf, red_src, red_buf, part, m_full,
     ab_buf, ab_part, wk_ref, wv_ref, wo_ref, rq_ref, cq_ref,
-    cell_sem, up_sem, in_sem, s_pr, r_pr, s_rs, r_rs, s_ag, r_ag, s_rx, r_rx, s_sm, r_sm, s_dt, r_dt,
+    cell_sem, up_sem, in_sem, out_sem, s_pr, r_pr, s_rs, r_rs, s_ag, r_ag, s_rx, r_rx, s_sm, r_sm, s_dt, r_dt,
     s_rd, r_rd, s_cx, r_cx, s_mg, r_mg, s_ab, r_ab, s_ac, r_ac,
 ):
     rows, cols, width = cells.shape
@@ -86,7 +87,7 @@
         copy.start()
     for k in range(n_chunk):
         local(cells_hbm, cells, cell_sem, k).start()
-    sub16 = lax.broadcasted_iota(jnp.int32, (16, width), 0)
+    sub16 = lax.broadcasted_iota(jnp.int32, (16, 2 * width), 0)
 
     barrier = pltpu.get_barrier_semaphore()
 
@@ -375,7 +376,7 @@
             hi = prod.astype(BF16)
             lo = (prod - hi.astype(F32)).astype(BF16)
             ones = jnp.where(sub16 == i, 1.0, 0.0).astype(BF16)
-            acc = acc + dot_nt(ones, hi) + dot_nt(ones, lo)
+            acc = acc + dot_nt(ones, jnp.concatenate([hi, lo], 1))
         cdp[at, :] = acc[0:chunk]
 
     part_dot = jnp.sum(wc[...] * cdp[...], 0, keepdims=True)
@@ -443,6 +444,25 @@
     half = jnp.concatenate([left, right], 1)
     base_out[...] = jnp.concatenate([half, half], 0)
 
+    owner = lax.rem(lax.broadcasted_iota(jnp.int32, base_out.shape, 0), rows)
+
+    def write(k):
+        at = pl.ds(k * chunk, chunk)
+        return pltpu.make_async_copy(up.at[at], raw_hbm.at[at], out_sem.at[k])
+
+    def cell_grads(first, last):
+        @pl.loop(first, last)
+        def _(k):
+            for i in range(chunk):
+                r = k * chunk + i
+                rhs = jnp.where(owner == r, base_out[...], 0.0).astype(BF16)
+                res = jnp.dot(lhs_out[...], rhs, preferred_element_type=F32)
+                delta = res[:, :width] + res[:, width:] * g_out[...]
+                up[r] = (up[r].astype(F32) + delta).astype(BF16)
+            write(k).start()
+
+    cell_grads(0, n_chunk // 2)
+
     wait_rows(*ab_x)
     acc = ab_buf[0]
     for i in range(1, n_row):
@@ -450,6 +470,7 @@
     ab_part[me_c] = acc
     ab_cx = (ab_part.at[me_c], ab_part, s_ac, r_ac)
     start_cols(*ab_cx)
+    cell_grads(n_chunk // 2, n_chunk)
     wait_rows(*collect)
     m_out[...] = jnp.concatenate([m_full[i, 0:m_per] for i in range(n_row)], 0)
     wait_cols(*ab_cx)
@@ -457,35 +478,35 @@
     for i in range(1, n_col):
         acc = acc + ab_part[i]
     ab_out[...] = acc
-
-
-def cell_kernel(
-    rows, lhs_ref, base_ref, g_ref, m_ref, ab_ref, wk_ref, wv_ref, wo_ref, rq_ref, cq_ref, up_ref,
-    out_ref, kwg_ref, vwg_ref, owg_ref, rqg_ref, cqg_ref,
+    for k in range(n_chunk):
+        write(k).wait()
+
+
+def finish_kernel(
+    pieces, raw_hbm, m_ref, ab_ref, wk_ref, wv_ref, wo_ref, rq_ref, cq_ref,
+    out_hbm, kwg_ref, vwg_ref, owg_ref, rqg_ref, cqg_ref, sems,
 ):
-    block = up_ref.shape[0]
-    width = up_ref.shape[2]
-    step = pl.program_id(0)
+    size = raw_hbm.shape[0] // pieces
+    width = m_ref.shape[0]
     scale = 1.0 / math.sqrt(width)
-    owner = lax.rem(lax.broadcasted_iota(jnp.int32, base_ref.shape, 0), rows)
-
-    @pl.when(step == 0)
-    def _():
-        ab, m = ab_ref[...], m_ref[...]
-        queries = jnp.concatenate([rq_ref[...], cq_ref[...], jnp.zeros((6, width), F32)], 0)
-        kwg_ref[...] = dot_tn(ab, queries * scale, HIGH)
-        q_grad = dot_nn(ab, wk_ref[...].astype(F32), HIGH) * scale
-        rqg_ref[...] = q_grad[0:1]
-        cqg_ref[...] = q_grad[1:2]
-        vwg_ref[...] = dot_nt(m, wo_ref[...].astype(F32), HIGH)
-        owg_ref[...] = dot_tn(wv_ref[...].astype(F32), m, HIGH)
-
-    @pl.loop(0, block, unroll=4)
-    def _(i):
-        rhs = jnp.where(owner == step * block + i, base_ref[...], 0.0).astype(BF16)
-        res = jnp.dot(lhs_ref[...], rhs, preferred_element_type=F32)
-        delta = res[:, :width] + res[:, width:] * g_ref[...]
-        out_ref[i] = (up_ref[i].astype(F32) + delta).astype(out_ref.dtype)
+    moves = [
+        pltpu.make_async_copy(
+            raw_hbm.at[pl.ds(i * size, size)], out_hbm.at[pl.ds(i * size, size)], sems.at[i]
+        )
+        for i in range(pieces)
+    ]
+    for move in moves:
+        move.start()
+    ab, m = ab_ref[...], m_ref[...]
+    queries = jnp.concatenate([rq_ref[...], cq_ref[...], jnp.zeros((6, width), F32)], 0)
+    kwg_ref[...] = dot_tn(ab, queries * scale, HIGH)
+    q_grad = dot_nn(ab, wk_ref[...].astype(F32), HIGH) * scale
+    rqg_ref[...] = q_grad[0:1]
+    cqg_ref[...] = q_grad[1:2]
+    vwg_ref[...] = dot_nt(m, wo_ref[...].astype(F32), HIGH)
+    owg_ref[...] = dot_tn(wv_ref[...].astype(F32), m, HIGH)
+    for move in moves:
+        move.wait()
 
 
 def on_device(n_row, n_col, cells, upstream, counts, wk, wv, wo, rq, cq):
@@ -504,18 +525,17 @@
     vector = jax.ShapeDtypeStruct((1, width), F32)
     half_n = n_row // 2
     over_row, over_col, over_chip = dma((n_row,)), dma((n_col,)), dma((half_n,))
-    lhs, base, g_col, m, ab = pl.pallas_call(
+    raw, m, ab = pl.pallas_call(
         functools.partial(stats_kernel, n_row, n_col, chunk),
         out_shape=(
-            jax.ShapeDtypeStruct((cols, 8 * rows), BF16),
-            jax.ShapeDtypeStruct((8 * rows, 2 * width), F32),
-            jax.ShapeDtypeStruct((cols, width), F32),
+            jax.ShapeDtypeStruct(cells.shape, BF16),
             square,
             jax.ShapeDtypeStruct((8, width), F32),
         ),
         in_specs=[hbm, hbm, pl.BlockSpec(memory_space=pltpu.SMEM)] + [hbm] * 5,
-        out_specs=(vmem,) * 5,
+        out_specs=(hbm, vmem, vmem),
         scratch_shapes=[
+            pltpu.VMEM((cols, 8 * rows), BF16), f32(8 * rows, 2 * width), f32(cols, width),
             pltpu.VMEM(cells.shape, BF16), pltpu.VMEM(cells.shape, BF16),
             f32(n_row, per, width), f32(half_n, per, width), f32(half_n, per, width),
             f32(half_n, per, width), f32(n_row, per, width),
@@ -530,7 +550,8 @@
             f32(n_row, 8, width), f32(n_col, 8, width),
             pltpu.VMEM(wk.shape, BF16), pltpu.VMEM(wv.shape, BF16), pltpu.VMEM(wo.shape, BF16),
             f32(1, width), f32(1, width),
-            dma((n_chunk,)), dma((n_chunk,)), dma((5,)), dma((2,)), dma((2,)),
+            dma((n_chunk,)), dma((n_chunk,)), dma((5,)), dma((n_chunk,)),
+            dma((2,)), dma((2,)),
             over_chip, over_chip, over_chip, over_chip,
             over_col, over_col, over_row, over_row, over_row, over_row,
             over_row, over_row, over_col, over_col, over_row, over_row,
@@ -541,22 +562,19 @@
         ),
         name="hub_stats",
     )(cells, upstream, counts, wk, wv, wo, rq, cq)
-    block = 8
-    whole = lambda shape: pl.BlockSpec(shape, lambda i: (0,) * len(shape))
-    cell_spec = pl.BlockSpec((block, cols, width), lambda i: (i, 0, 0))
-    fixed = (lhs, base, g_col, m, ab, wk, wv, wo, rq, cq)
+    pieces = 16
     cell_grad, kwg, vwg, owg, rqg, cqg = pl.pallas_call(
-        functools.partial(cell_kernel, rows),
-        grid=(rows // block,),
+        functools.partial(finish_kernel, pieces),
         out_shape=(
             jax.ShapeDtypeStruct(cells.shape, cells.dtype),
             square, square, square, vector, vector,
         ),
-        in_specs=[whole(x.shape) for x in fixed] + [cell_spec],
-        out_specs=(cell_spec,) + (whole((width, width)),) * 3 + (whole((1, width)),) * 2,
+        in_specs=[hbm] + [vmem] * 7,
+        out_specs=(hbm,) + (vmem,) * 5,
+        scratch_shapes=[dma((pieces,))],
         compiler_params=pltpu.CompilerParams(vmem_limit_bytes=VMEM_BYTES),
-        name="cell_grad",
-    )(*fixed, upstream)
+        name="finish",
+    )(raw, m, ab, wk, wv, wo, rq, cq)
     return cell_grad, kwg, vwg, owg, rqg.reshape(width), cqg.reshape(width)
 
 

time: 48.2 us -> 170 us (3.53)
  Pallas kernels: 47.4 us -> 169 us
    pallas_call x1, Pallas kernels: 7.5 us -> 130 us  [on_device(): pl.pallas_call(functools.partial(finish_kernel, pieces), out_shape=(jax.S...]
where the time goes in v2:
time: 170 us
  Pallas kernels  169 us (99%)
    pallas_call x1, Pallas kernels, on_device(): pl.pallas_call(functools.partial(finish_kernel, pieces), out_shape=(jax.S...  130 us
    pallas_call x1, Pallas kernels, on_device(): pl.pallas_call(functools.partial(stats_kernel, n_row, n_col, chunk), out_...  39.6 us

profile of v2, /device:TPU:0, one launch (start us, length us, event | category | flops | bytes accessed | tf_op | source)
XLA Modules:
  0.0 170.1 jit_solution(16720994594963900452)
XLA Ops:
  0.6 39.6 %hub_stats.1 = (bf16[32,512,128]{2,1,0:T(8,128)(2,1)}, f32[128,128]{1,0:T(8,128)}, f32[8,128]{1,0:T(8,128)}) custom-call(bf16[32,512,128]{2,1,0:T(8,128)(2,1)} %cells_hbm.1, bf16[32,512,128]{2,1,0:T(8,128)(2,1)} %up_hbm.1, s32[32]{0:T(128)} %counts.1, bf16[128,128]{1,0:T(8,128)(2,1)} %wk_ref.1, bf16[128,128]{1,0:T(8,128)(2,1)} %wv_ref.1, ...), custom_call_target="tpu_custom_call" | custom-call | tf_op jit(solution)/shard_map/hub_stats/pallas_call | solution.py:528
  40.2 129.9 %finish.1 = (bf16[32,512,128]{2,1,0:T(8,128)(2,1)}, f32[128,128]{1,0:T(8,128)}, f32[128,128]{1,0:T(8,128)}, f32[128,128]{1,0:T(8,128)}, f32[1,128]{1,0:T(1,128)}, /*index=5*/f32[1,128]{1,0:T(1,128)}) custom-call(bf16[32,512,128]{2,1,0:T(8,128)(2,1)} %get-tuple-element.15.raw_hbm, f32[128,128]{1,0:T(8,128)} %get-tuple-element.16.m_ref, ...), custom_call_target="tpu_custom_call" | custom-call | tf_op jit(solution)/shard_map/finish/pallas_call | solution.py:566

commit v3 on v2

--- a/solution.py
+++ b/solution.py
@@ -484,19 +484,25 @@
 
 def finish_kernel(
     pieces, raw_hbm, m_ref, ab_ref, wk_ref, wv_ref, wo_ref, rq_ref, cq_ref,
-    out_hbm, kwg_ref, vwg_ref, owg_ref, rqg_ref, cqg_ref, sems,
+    out_hbm, kwg_ref, vwg_ref, owg_ref, rqg_ref, cqg_ref, stage, in_sem, out_sem,
 ):
     size = raw_hbm.shape[0] // pieces
     width = m_ref.shape[0]
     scale = 1.0 / math.sqrt(width)
-    moves = [
-        pltpu.make_async_copy(
-            raw_hbm.at[pl.ds(i * size, size)], out_hbm.at[pl.ds(i * size, size)], sems.at[i]
-        )
-        for i in range(pieces)
-    ]
-    for move in moves:
-        move.start()
+    pairs = []
+    for i in range(pieces):
+        at = pl.ds(i * size, size)
+        pairs.append(
+            (
+                pltpu.make_async_copy(raw_hbm.at[at], stage.at[at], in_sem.at[i]),
+                pltpu.make_async_copy(stage.at[at], out_hbm.at[at], out_sem.at[i]),
+            )
+        )
+    for load, _ in pairs:
+        load.start()
+    for load, store in pairs:
+        load.wait()
+        store.start()
     ab, m = ab_ref[...], m_ref[...]
     queries = jnp.concatenate([rq_ref[...], cq_ref[...], jnp.zeros((6, width), F32)], 0)
     kwg_ref[...] = dot_tn(ab, queries * scale, HIGH)
@@ -505,8 +511,8 @@
     cqg_ref[...] = q_grad[1:2]
     vwg_ref[...] = dot_nt(m, wo_ref[...].astype(F32), HIGH)
     owg_ref[...] = dot_tn(wv_ref[...].astype(F32), m, HIGH)
-    for move in moves:
-        move.wait()
+    for _, store in pairs:
+        store.wait()
 
 
 def on_device(n_row, n_col, cells, upstream, counts, wk, wv, wo, rq, cq):
@@ -562,7 +568,7 @@
         ),
         name="hub_stats",
     )(cells, upstream, counts, wk, wv, wo, rq, cq)
-    pieces = 16
+    pieces = 8
     cell_grad, kwg, vwg, owg, rqg, cqg = pl.pallas_call(
         functools.partial(finish_kernel, pieces),
         out_shape=(
@@ -571,7 +577,7 @@
         ),
         in_specs=[hbm] + [vmem] * 7,
         out_specs=(hbm,) + (vmem,) * 5,
-        scratch_shapes=[dma((pieces,))],
+        scratch_shapes=[pltpu.VMEM(cells.shape, BF16), dma((pieces,)), dma((pieces,))],
         compiler_params=pltpu.CompilerParams(vmem_limit_bytes=VMEM_BYTES),
         name="finish",
     )(raw, m, ab, wk, wv, wo, rq, cq)

time: 170 us -> 45.5 us (0.27)
  Pallas kernels: 169 us -> 44.7 us
    pallas_call x1, Pallas kernels: 130 us -> 5.14 us  [on_device(): pl.pallas_call(functools.partial(finish_kernel, pieces), out_shape=(jax.S...]
where the time goes in v3:
time: 45.5 us; the launch traced here: 45.4 us
  Pallas kernels  44.7 us (98%)
  between operations  0.64 us (1%)
    pallas_call x1, Pallas kernels, on_device(): pl.pallas_call(functools.partial(stats_kernel, n_row, n_col, chunk), out_...  39.6 us
    pallas_call x1, Pallas kernels, on_device(): pl.pallas_call(functools.partial(finish_kernel, pieces), out_shape=(jax.S...  5.14 us

profile of v3, /device:TPU:0, one launch (start us, length us, event | category | flops | bytes accessed | tf_op | source)
XLA Modules:
  0.0 45.4 jit_solution(1801425116865301057)
XLA Ops:
  0.6 39.6 %hub_stats.1 = (bf16[32,512,128]{2,1,0:T(8,128)(2,1)}, f32[128,128]{1,0:T(8,128)}, f32[8,128]{1,0:T(8,128)}) custom-call(bf16[32,512,128]{2,1,0:T(8,128)(2,1)} %cells_hbm.1, bf16[32,512,128]{2,1,0:T(8,128)(2,1)} %up_hbm.1, s32[32]{0:T(128)} %counts.1, bf16[128,128]{1,0:T(8,128)(2,1)} %wk_ref.1, bf16[128,128]{1,0:T(8,128)(2,1)} %wv_ref.1, ...), custom_call_target="tpu_custom_call" | custom-call | tf_op jit(solution)/shard_map/hub_stats/pallas_call | solution.py:534
  40.2 5.1 %finish.1 = (bf16[32,512,128]{2,1,0:T(8,128)(2,1)}, f32[128,128]{1,0:T(8,128)}, f32[128,128]{1,0:T(8,128)}, f32[128,128]{1,0:T(8,128)}, f32[1,128]{1,0:T(1,128)}, /*index=5*/f32[1,128]{1,0:T(1,128)}) custom-call(bf16[32,512,128]{2,1,0:T(8,128)(2,1)} %get-tuple-element.15.raw_hbm, f32[128,128]{1,0:T(8,128)} %get-tuple-element.16.m_ref, ...), custom_call_target="tpu_custom_call" | custom-call | tf_op jit(solution)/shard_map/finish/pallas_call | solution.py:572

commit v4 on v2

--- a/solution.py
+++ b/solution.py
@@ -354,16 +354,6 @@
     other_at = cot_full.at[pl.ds(other, half_n)]
     to_sibling(other_at, other_at, s_pr.at[1], r_pr.at[1]).wait_recv()
     cot_all = cot_full[...].reshape(cols, width)
-    m_loc = dot_tn(col_pool[...] * f_t, cot_all, HIGH)
-    m_loc = m_loc + dot_tn(row_pool[...] * factor, cot, HIGH)
-    for i in range(n_row):
-        red_src[i, 0:m_per] = m_loc[i * m_per : (i + 1) * m_per]
-        if m_per < 8:
-            red_src[i, m_per:8] = jnp.zeros((8 - m_per, width), F32)
-    reduce = (lambda peer: red_src.at[peer], red_buf, s_rd, r_rd)
-    start_rows(*reduce)
-    red_buf[me_r] = red_src[me_r]
-
     g_col = dot_nt(cot_all, both, HIGH)
     g_out[...] = g_col
 
@@ -385,13 +375,24 @@
     dots_x = (lambda peer: dots_buf.at[me_r], dots_buf, s_dt, r_dt)
     start_rows(*dots_x)
 
-    wait_rows(*reduce)
-    acc = red_buf[0]
-    for i in range(1, n_row):
-        acc = acc + red_buf[i]
-    part[me_c] = acc
-    col_x = (part.at[me_c], part, s_cx, r_cx)
-    start_cols(*col_x)
+    m_loc = dot_tn(col_pool[...] * f_t, cot_all, HIGH)
+    m_loc = m_loc + dot_tn(row_pool[...] * factor, cot, HIGH)
+    for i in range(n_row):
+        red_src[i, 0:m_per] = m_loc[i * m_per : (i + 1) * m_per]
+        if m_per < 8:
+            red_src[i, m_per:8] = jnp.zeros((8 - m_per, width), F32)
+    reduce = (lambda peer: red_src.at[peer], red_buf, s_rd, r_rd)
+    start_rows(*reduce)
+    red_buf[me_r] = red_src[me_r]
+
+    zero = jnp.zeros((rows, width), F32)
+    one = jnp.ones((rows, width), F32)
+    left = jnp.concatenate(
+        [g_row, jnp.broadcast_to(kr, (rows, width)), jnp.broadcast_to(kc, (rows, width)), zero], 0
+    )
+    right = jnp.concatenate([zero, zero, zero, one], 0)
+    half = jnp.concatenate([left, right], 1)
+    base_out[...] = jnp.concatenate([half, half], 0)
 
     wait_rows(*dots_x)
     dots = dots_buf[0, 0:q_rows]
@@ -423,27 +424,18 @@
     ab_x = (lambda peer: ab_buf.at[me_r], ab_buf, s_ab, r_ab)
     start_rows(*ab_x)
 
-    wait_cols(*col_x)
-    acc = part[0]
-    for i in range(1, n_col):
-        acc = acc + part[i]
-    m_full[me_r] = acc
-    collect = (lambda peer: m_full.at[me_r], m_full, s_mg, r_mg)
-    start_rows(*collect)
+    wait_rows(*reduce)
+    acc = red_buf[0]
+    for i in range(1, n_row):
+        acc = acc + red_buf[i]
+    part[me_c] = acc
+    col_x = (part.at[me_c], part, s_cx, r_cx)
+    start_cols(*col_x)
 
     pieces = [split(x, 2) for x in (row_prob, row_ds, col_ds, wc[...])]
     for half in range(2):
         block = jnp.concatenate([p[half] for p in pieces], 0)
         lhs_out[:, half * 4 * rows : (half + 1) * 4 * rows] = block.T.astype(BF16)
-    zero = jnp.zeros((rows, width), F32)
-    one = jnp.ones((rows, width), F32)
-    left = jnp.concatenate(
-        [g_row, jnp.broadcast_to(kr, (rows, width)), jnp.broadcast_to(kc, (rows, width)), zero], 0
-    )
-    right = jnp.concatenate([zero, zero, zero, one], 0)
-    half = jnp.concatenate([left, right], 1)
-    base_out[...] = jnp.concatenate([half, half], 0)
-
     owner = lax.rem(lax.broadcasted_iota(jnp.int32, base_out.shape, 0), rows)
 
     def write(k):
@@ -461,7 +453,15 @@
                 up[r] = (up[r].astype(F32) + delta).astype(BF16)
             write(k).start()
 
-    cell_grads(0, n_chunk // 2)
+    cell_grads(0, n_chunk // 4)
+    wait_cols(*col_x)
+    acc = part[0]
+    for i in range(1, n_col):
+        acc = acc + part[i]
+    m_full[me_r] = acc
+    collect = (lambda peer: m_full.at[me_r], m_full, s_mg, r_mg)
+    start_rows(*collect)
+    cell_grads(n_chunk // 4, n_chunk // 2)
 
     wait_rows(*ab_x)
     acc = ab_buf[0]
@@ -483,30 +483,59 @@
 
 
 def finish_kernel(
-    pieces, raw_hbm, m_ref, ab_ref, wk_ref, wv_ref, wo_ref, rq_ref, cq_ref,
-    out_hbm, kwg_ref, vwg_ref, owg_ref, rqg_ref, cqg_ref, sems,
+    pieces, raw_hbm, m_hbm, ab_hbm, wk_hbm, wv_hbm, wo_hbm, rq_hbm, cq_hbm,
+    out_hbm, kwg_hbm, vwg_hbm, owg_hbm, rqg_hbm, cqg_hbm,
+    stage, m_ref, ab_ref, wk_ref, wv_ref, wo_ref, rq_ref, cq_ref,
+    kwg_ref, vwg_ref, owg_ref, rqg_ref, cqg_ref, in_sem, out_sem, arg_sem, res_sem,
 ):
     size = raw_hbm.shape[0] // pieces
     width = m_ref.shape[0]
     scale = 1.0 / math.sqrt(width)
-    moves = [
-        pltpu.make_async_copy(
-            raw_hbm.at[pl.ds(i * size, size)], out_hbm.at[pl.ds(i * size, size)], sems.at[i]
-        )
-        for i in range(pieces)
-    ]
-    for move in moves:
-        move.start()
+
+    def copies(sources, targets, sem):
+        return [
+            pltpu.make_async_copy(src, dst, sem.at[i])
+            for i, (src, dst) in enumerate(zip(sources, targets))
+        ]
+
+    arguments = copies(
+        (m_hbm, ab_hbm, wk_hbm, wv_hbm, wo_hbm, rq_hbm, cq_hbm),
+        (m_ref, ab_ref, wk_ref, wv_ref, wo_ref, rq_ref, cq_ref),
+        arg_sem,
+    )
+    results = copies(
+        (kwg_ref, vwg_ref, owg_ref, rqg_ref, cqg_ref),
+        (kwg_hbm, vwg_hbm, owg_hbm, rqg_hbm, cqg_hbm),
+        res_sem,
+    )
+    parts = [pl.ds(i * size, size) for i in range(pieces)]
+    loads = copies([raw_hbm.at[p] for p in parts], [stage.at[p] for p in parts], in_sem)
+    stores = copies([stage.at[p] for p in parts], [out_hbm.at[p] for p in parts], out_sem)
+    for copy in arguments + loads:
+        copy.start()
+
+    def forward(first, last):
+        for i in range(first, last):
+            loads[i].wait()
+            stores[i].start()
+
+    for copy in arguments:
+        copy.wait()
+    forward(0, pieces // 4)
     ab, m = ab_ref[...], m_ref[...]
     queries = jnp.concatenate([rq_ref[...], cq_ref[...], jnp.zeros((6, width), F32)], 0)
     kwg_ref[...] = dot_tn(ab, queries * scale, HIGH)
     q_grad = dot_nn(ab, wk_ref[...].astype(F32), HIGH) * scale
     rqg_ref[...] = q_grad[0:1]
     cqg_ref[...] = q_grad[1:2]
+    forward(pieces // 4, pieces // 2)
     vwg_ref[...] = dot_nt(m, wo_ref[...].astype(F32), HIGH)
+    forward(pieces // 2, pieces)
     owg_ref[...] = dot_tn(wv_ref[...].astype(F32), m, HIGH)
-    for move in moves:
-        move.wait()
+    for copy in results:
+        copy.start()
+    for copy in stores + results:
+        copy.wait()
 
 
 def on_device(n_row, n_col, cells, upstream, counts, wk, wv, wo, rq, cq):
@@ -562,16 +591,22 @@
         ),
         name="hub_stats",
     )(cells, upstream, counts, wk, wv, wo, rq, cq)
-    pieces = 16
+    pieces = 8
     cell_grad, kwg, vwg, owg, rqg, cqg = pl.pallas_call(
         functools.partial(finish_kernel, pieces),
         out_shape=(
             jax.ShapeDtypeStruct(cells.shape, cells.dtype),
             square, square, square, vector, vector,
         ),
-        in_specs=[hbm] + [vmem] * 7,
-        out_specs=(hbm,) + (vmem,) * 5,
-        scratch_shapes=[dma((pieces,))],
+        in_specs=[hbm] * 8,
+        out_specs=(hbm,) * 6,
+        scratch_shapes=[
+            pltpu.VMEM(cells.shape, BF16), f32(width, width), f32(8, width),
+            pltpu.VMEM(wk.shape, BF16), pltpu.VMEM(wv.shape, BF16), pltpu.VMEM(wo.shape, BF16),
+            f32(1, width), f32(1, width),
+            f32(width, width), f32(width, width), f32(width, width), f32(1, width), f32(1, width),
+            dma((pieces,)), dma((pieces,)), dma((7,)), dma((5,)),
+        ],
         compiler_params=pltpu.CompilerParams(vmem_limit_bytes=VMEM_BYTES),
         name="finish",
     )(raw, m, ab, wk, wv, wo, rq, cq)

time: 170 us -> 44.9 us (0.26)
  Pallas kernels: 169 us -> 44.1 us
    pallas_call x1, Pallas kernels: 130 us -> 4.13 us  [on_device(): pl.pallas_call(functools.partial(finish_kernel, pieces), out_shape=(jax.S...]
where the time goes in v4:
time: 44.9 us; the launch traced here: 44.7 us
  Pallas kernels  44.1 us (98%)
  between operations  0.64 us (1%)
    pallas_call x1, Pallas kernels, on_device(): pl.pallas_call(functools.partial(stats_kernel, n_row, n_col, chunk), out_...  40 us
    pallas_call x1, Pallas kernels, on_device(): pl.pallas_call(functools.partial(finish_kernel, pieces), out_shape=(jax.S...  4.13 us

profile of v4, /device:TPU:0, one launch (start us, length us, event | category | flops | bytes accessed | tf_op | source)
XLA Modules:
  0.0 44.7 jit_solution(11618775035596619770)
XLA Ops:
  0.6 40.0 %hub_stats.1 = (bf16[32,512,128]{2,1,0:T(8,128)(2,1)}, f32[128,128]{1,0:T(8,128)}, f32[8,128]{1,0:T(8,128)}) custom-call(bf16[32,512,128]{2,1,0:T(8,128)(2,1)} %cells_hbm.1, bf16[32,512,128]{2,1,0:T(8,128)(2,1)} %up_hbm.1, s32[32]{0:T(128)} %counts.1, bf16[128,128]{1,0:T(8,128)(2,1)} %wk_hbm.3, bf16[128,128]{1,0:T(8,128)(2,1)} %wv_hbm.3, ...), custom_call_target="tpu_custom_call" | custom-call | tf_op jit(solution)/shard_map/hub_stats/pallas_call | solution.py:557
  40.6 4.1 %finish.1 = (bf16[32,512,128]{2,1,0:T(8,128)(2,1)}, f32[128,128]{1,0:T(8,128)}, f32[128,128]{1,0:T(8,128)}, f32[128,128]{1,0:T(8,128)}, f32[1,128]{1,0:T(1,128)}, /*index=5*/f32[1,128]{1,0:T(1,128)}) custom-call(bf16[32,512,128]{2,1,0:T(8,128)(2,1)} %get-tuple-element.15.raw_hbm, f32[128,128]{1,0:T(8,128)} %get-tuple-element.16.m_hbm, ...), custom_call_target="tpu_custom_call" | custom-call | tf_op jit(solution)/shard_map/finish/pallas_call | solution.py:595

commit v5 on v4

--- a/solution.py
+++ b/solution.py
@@ -191,7 +191,7 @@
             return total + jnp.sum(x, 1)
 
         row_cot[pl.ds(k * chunk, chunk), :] = lax.fori_loop(
-            0, cols // span, add_block, jnp.zeros((chunk, width), F32)
+            0, cols // span, add_block, jnp.zeros((chunk, width), F32), unroll=2
         )
 
     pl.semaphore_wait(barrier, n_row + n_col - 2)
@@ -279,23 +279,6 @@
     row_buf[me_c, 3] = jnp.broadcast_to(row_t, (rows, width))
     row_x = (row_buf.at[me_c], row_buf, s_rx, r_rx)
     start_cols(*row_x)
-
-    w_t = jnp.concatenate([p.T for p in split(weight, 2)], 1).astype(BF16)
-    pick = lax.rem(lax.broadcasted_iota(jnp.int32, (2 * rows, 2 * width), 0), rows)
-    lane = lax.broadcasted_iota(jnp.int32, (2 * rows, 2 * width), 1)
-    pick = pick - jnp.where(lane < width, 0, 1)
-    col_pool[...] = jnp.zeros_like(col_pool)
-
-    @pl.loop(0, rows // 4)
-    def _(k):
-        acc = col_pool[...]
-        for i in (0, 2):
-            r = k * 4 + i
-            one = jnp.where(pick == r, 1.0, 0.0).astype(BF16)
-            spread = jnp.dot(w_t, one, preferred_element_type=F32)
-            acc = acc + spread[:, :width] * cells[r].astype(F32)
-            acc = acc + spread[:, width:] * cells[r + 1].astype(F32)
-        col_pool[...] = acc
 
     wait_cols(*row_x)
     top = row_buf[0, 2]
@@ -374,6 +357,23 @@
         dots_buf[me_r, pl.ds(i, 1), :] = part_dot[:, i * 128 : (i + 1) * 128]
     dots_x = (lambda peer: dots_buf.at[me_r], dots_buf, s_dt, r_dt)
     start_rows(*dots_x)
+
+    w_t = jnp.concatenate([p.T for p in split(weight, 2)], 1).astype(BF16)
+    pick = lax.rem(lax.broadcasted_iota(jnp.int32, (2 * rows, 2 * width), 0), rows)
+    lane = lax.broadcasted_iota(jnp.int32, (2 * rows, 2 * width), 1)
+    pick = pick - jnp.where(lane < width, 0, 1)
+    col_pool[...] = jnp.zeros_like(col_pool)
+
+    @pl.loop(0, rows // 4)
+    def _(k):
+        acc = col_pool[...]
+        for i in (0, 2):
+            r = k * 4 + i
+            one = jnp.where(pick == r, 1.0, 0.0).astype(BF16)
+            spread = jnp.dot(w_t, one, preferred_element_type=F32)
+            acc = acc + spread[:, :width] * cells[r].astype(F32)
+            acc = acc + spread[:, width:] * cells[r + 1].astype(F32)
+        col_pool[...] = acc
 
     m_loc = dot_tn(col_pool[...] * f_t, cot_all, HIGH)
     m_loc = m_loc + dot_tn(row_pool[...] * factor, cot, HIGH)

time: 44.9 us -> 45.6 us (1.016)
  Pallas kernels: 44.1 us -> 44.9 us
    pallas_call x1, Pallas kernels: 40 us -> 40.7 us  [on_device(): pl.pallas_call(functools.partial(stats_kernel, n_row, n_col, chunk), out_...]
where the time goes in v5:
time: 45.6 us; the launch traced here: 45.5 us
  Pallas kernels  44.9 us (98%)
  between operations  0.64 us (1%)
    pallas_call x1, Pallas kernels, on_device(): pl.pallas_call(functools.partial(stats_kernel, n_row, n_col, chunk), out_...  40.7 us
    pallas_call x1, Pallas kernels, on_device(): pl.pallas_call(functools.partial(finish_kernel, pieces), out_shape=(jax.S...  4.13 us

profile of v5, /device:TPU:0, one launch (start us, length us, event | category | flops | bytes accessed | tf_op | source)
XLA Modules:
  0.0 45.5 jit_solution(7992892188424292586)
XLA Ops:
  0.6 40.7 %hub_stats.1 = (bf16[32,512,128]{2,1,0:T(8,128)(2,1)}, f32[128,128]{1,0:T(8,128)}, f32[8,128]{1,0:T(8,128)}) custom-call(bf16[32,512,128]{2,1,0:T(8,128)(2,1)} %cells_hbm.1, bf16[32,512,128]{2,1,0:T(8,128)(2,1)} %up_hbm.1, s32[32]{0:T(128)} %counts.1, bf16[128,128]{1,0:T(8,128)(2,1)} %wk_hbm.3, bf16[128,128]{1,0:T(8,128)(2,1)} %wv_hbm.3, ...), custom_call_target="tpu_custom_call" | custom-call | tf_op jit(solution)/shard_map/hub_stats/pallas_call | solution.py:557
  41.4 4.1 %finish.1 = (bf16[32,512,128]{2,1,0:T(8,128)(2,1)}, f32[128,128]{1,0:T(8,128)}, f32[128,128]{1,0:T(8,128)}, f32[128,128]{1,0:T(8,128)}, f32[1,128]{1,0:T(1,128)}, /*index=5*/f32[1,128]{1,0:T(1,128)}) custom-call(bf16[32,512,128]{2,1,0:T(8,128)(2,1)} %get-tuple-element.15.raw_hbm, f32[128,128]{1,0:T(8,128)} %get-tuple-element.16.m_hbm, ...), custom_call_target="tpu_custom_call" | custom-call | tf_op jit(solution)/shard_map/finish/pallas_call | solution.py:595
